TPU v7x, 128 devices: a whole 4x4x4 slice. The times are simulated.
128 devices in a mesh: section: 2 (over core), dp: 64 (over y, x, z).
Axes of the slice: x: 4, y: 4, z: 4, core: 2. Of those that a mesh axis runs over, the one named last changes fastest.
Arguments:
- tokens: bfloat16 [128, 64, 768], P('dp', 'section'), may hold values from -6 to 6
- out_grad: bfloat16 [128, 64, 768], P('dp', 'section'), may hold values from -6 to 6
- passes: int32 [128], P('dp'), may hold values from 2 to 5
- pass_embed: float32 [5, 768], replicated, may hold values from -3 to 3
- qkv_weight: bfloat16 [2, 768, 2304], P('section'), may hold values from -0.21875 to 0.21875
- out_weight: bfloat16 [2, 768, 768], P('section'), may hold values from -0.875 to 0.875
- up_weight: bfloat16 [2, 768, 3072], P('section'), may hold values from -0.21875 to 0.21875
- down_weight: bfloat16 [2, 3072, 768], P('section'), may hold values from -0.109375 to 0.109375
- norm_gains: float32 [2, 2, 768], P('section'), may hold values from 0.1 to 1.9
- bias_rows: float32 [2, 6, 768], P('section'), may hold values from -1.8 to 1.8
- up_bias: float32 [2, 3072], P('section'), may hold values from -1.8 to 1.8
Outputs:
- hidden_out: bfloat16 [128, 64, 768], P('dp', 'section')
- token_grad: bfloat16 [128, 64, 768], P('dp', 'section')
- grad_qkv_weight: float32 [2, 768, 2304], P('section', 'dp')
- grad_out_weight: float32 [2, 768, 768], P('section', 'dp')
- grad_up_weight: float32 [2, 768, 3072], P('section', 'dp')
- grad_down_weight: float32 [2, 3072, 768], P('section', 'dp')
- grad_norm_gains: float32 [2, 2, 768], P('section', None, 'dp')
- grad_bias_rows: float32 [2, 6, 768], P('section', None, 'dp')
- grad_up_bias: float32 [2, 3072], P('section', 'dp')
- grad_pass_embed: float32 [5, 768], P(None, ('section', 'dp'))
All inputs are finite; a program needn't handle non-finite values.
Results may differ from a plain program's by a relative error of at most 0.017.
Values may be sent and summed in bfloat16 or wider, within the bound.
A program may use at most 256 MiB of HBM per device.

v0:
```python
import jax
import jax.numpy as jnp
import numpy as np
from jax import lax
from jax.experimental import pallas as pl
from jax.experimental.pallas import tpu as pltpu
from jax.sharding import PartitionSpec as P

F32 = jnp.float32
BF16 = jnp.bfloat16
VM = pltpu.VMEM
MESH = pl.DeviceIdType.MESH
D = 768
FF = 3072
SEQ = 64
R = 2 * SEQ
SLOTS = 4
ROWS = SLOTS * R
STEP = 256
KEYS = SLOTS * SEQ
STRIDE = {"y": 16, "x": 4, "z": 1}
Q, U, W = 0, 1, 2
AXES = ("x", "z", "y")


class Names:
    def __init__(self, **entries):
        self.__dict__.update(entries)


def nn(a, b):
    return jnp.dot(a, b, preferred_element_type=F32)


def nt(a, b):
    return lax.dot_general(a, b, (((1,), (1,)), ((), ())), preferred_element_type=F32)


def tn(a, b):
    return lax.dot_general(a, b, (((0,), (0,)), ((), ())), preferred_element_type=F32)


def lane_masks(value, dtype):
    lane = lax.broadcasted_iota(jnp.int32, (1, STEP), 1) // 64
    return [jnp.where(lane == h, value, 0.0).astype(dtype) for h in range(4)]


def norm_forward(u, gain, shift, hat_ref, inv_ref):
    out = []
    for r in range(0, R, 32):
        v = u[r:r + 32]
        centre = v - jnp.sum(v, -1, keepdims=True) * (1.0 / D)
        inv = lax.rsqrt(jnp.sum(centre * centre, -1, keepdims=True) * (1.0 / D) + 1e-5)
        hat = centre * inv
        hat_ref[r:r + 32] = hat
        inv_ref[r:r + 32] = jnp.broadcast_to(inv, (32, 128))
        out.append((hat * gain + shift).astype(BF16))
    return jnp.concatenate(out, 0)


def norm_backward(dy, gain, hat_ref, inv_ref):
    out, dgain, dshift = [], 0.0, 0.0
    for r in range(0, R, 32):
        g = dy[r:r + 32]
        hat = hat_ref[r:r + 32]
        inv = inv_ref[r:r + 32][:, :1]
        dgain = dgain + jnp.sum(g * hat, 0, keepdims=True)
        dshift = dshift + jnp.sum(g, 0, keepdims=True)
        gg = g * gain
        m1 = jnp.sum(gg, -1, keepdims=True) * (1.0 / D)
        m2 = jnp.sum(gg * hat, -1, keepdims=True) * (1.0 / D)
        out.append((gg - m1 - hat * m2) * inv)
    return jnp.concatenate(out, 0), dgain, dshift


def forward(j, u, w, p, s):
    rows = pl.ds(pl.multiple_of(j * R, R), R)
    slot = pl.ds(pl.multiple_of(j * SEQ, SEQ), SEQ)
    a = norm_forward(u, p.gain(0), p.bias(0), s.hat1.at[j], s.inv1.at[j])
    s.ao[0, rows] = a
    for n in range(0, 3 * D, STEP):
        k = n % D
        if k == 0:
            w.wait(j, n // D)
        c = nn(a, w.qkv[n // D, :, k:k + STEP])
        if n < D:
            s.dcz[rows, k:k + STEP] = (c + p.bias(1)[:, k:k + STEP]).astype(BF16)
        elif n < 2 * D:
            c = c.astype(BF16)
            for q in range(2):
                s.k[q, slot, k:k + STEP] = c[q * SEQ:(q + 1) * SEQ]
        else:
            c = (c + p.bias(2)[:, k:k + STEP]).astype(BF16)
            for q in range(2):
                s.v[q, slot, k:k + STEP] = c[q * SEQ:(q + 1) * SEQ]
    w.done(j, 0)
    ones = lane_masks(1.0, F32)
    eighth = lane_masks(0.125, BF16)
    col = lax.broadcasted_iota(jnp.int32, (SEQ, KEYS), 1)
    row = lax.broadcasted_iota(jnp.int32, (SEQ, KEYS), 0)
    allow = ((col & 63) <= row) & (col < (j + 1) * SEQ)
    veto = jnp.where(allow, 0.0, -1e30)
    veto = jnp.concatenate([veto] * 4, 0)
    for q in range(2):
        qrows = pl.ds(pl.multiple_of(j * R + q * SEQ, SEQ), SEQ)
        for g in range(3):
            cols = slice(g * STEP, (g + 1) * STEP)
            q4 = s.dcz[qrows, cols]
            q4 = jnp.concatenate([q4 * m for m in eighth], 0)
            sc = nt(q4, s.k[q, :, cols]) + veto
            ex = jnp.exp(sc - jnp.max(sc, -1, keepdims=True))
            pr = ex * (1.0 / jnp.sum(ex, -1, keepdims=True))
            s.p[j, 3 * q + g] = pr
            o4 = nn(pr.astype(BF16), s.v[q, :, cols])
            o = sum(o4[h * SEQ:(h + 1) * SEQ] * ones[h] for h in range(4))
            s.ao[1, qrows, cols] = o.astype(BF16)
    s.post(0, Q, j)
    o = s.ao[1, rows]
    w.wait(j, 3)
    m1 = u + (jnp.concatenate([nn(o, w.out[:, n:n + STEP]) for n in range(0, D, STEP)], 1) + p.bias(3))
    w.done(j, 1)
    b = norm_forward(m1, p.gain(1), p.bias(4), s.hat2.at[j], s.inv2.at[j])
    s.b[rows] = b
    s.post(0, U, j)
    w.wait(j, 4)
    for n in range(0, FF, STEP):
        f = nn(b, w.up[:, n:n + STEP]) + p.up(n, n + STEP)
        ff = f * f
        half = 0.5 + 0.5 * jnp.tanh(f * (0.7978845608 + (0.7978845608 * 0.044715) * ff))
        e = f * half
        s.e[rows, n:n + STEP] = e.astype(BF16)
        s.slope[j, :, n:n + STEP] = half + e * (1.0 - half) * (
            2 * 0.7978845608 + (6 * 0.7978845608 * 0.044715) * ff)
    w.done(j, 2)
    s.post(0, W, j)
    e = s.e[rows]
    w.wait(j, 5)
    r = jnp.concatenate([nn(e, w.down[:, n:n + STEP]) for n in range(0, D, STEP)], 1)
    w.done(j, 3)
    return m1 + (r + p.bias(5))


def backward(j, dr, w, p, s, t):
    rows = pl.ds(pl.multiple_of(j * R, R), R)
    slot = pl.ds(pl.multiple_of(j * SEQ, SEQ), SEQ)
    dr2 = dr.astype(BF16)
    s.dr[rows] = dr2
    s.post(1, W, j)
    t.add(2 + 5, jnp.sum(dr, 0, keepdims=True))
    w.ready(j, 2)
    for n in range(0, FF, STEP):
        de = nn(dr2, w.up[:, n:n + STEP])
        df = s.slope[j, :, n:n + STEP] * de
        t.add(12 + n // D, jnp.sum(df, 0, keepdims=True), n % D)
        s.df[rows, n:n + STEP] = df.astype(BF16)
    s.post(1, U, j)
    df = s.df[rows]
    w.ready(j, 3)
    db = jnp.concatenate([nn(df, w.down[:, n:n + STEP]) for n in range(0, D, STEP)], 1)
    dm, dgain, dshift = norm_backward(db, p.gain(1), s.hat2.at[j], s.inv2.at[j])
    t.add(1, dgain)
    t.add(2 + 4, dshift)
    dm1 = dr + dm
    dz = dm1.astype(BF16)
    s.dcz[rows, 3 * D:] = dz
    t.add(2 + 3, jnp.sum(dm1, 0, keepdims=True))
    w.ready(j, 1)
    for n in range(0, D, STEP):
        s.dcz[rows, 2 * D + n:2 * D + n + STEP] = nn(dz, w.out[:, n:n + STEP]).astype(BF16)
    ones = lane_masks(1.0, BF16)
    eighth = lane_masks(0.125, BF16)
    eighth32 = lane_masks(0.125, F32)
    for q in range(2):
        drows = pl.ds(pl.multiple_of(j * R + q * SEQ, SEQ), SEQ)
        for g in range(3):
            cols = slice(g * STEP, (g + 1) * STEP)
            do4 = s.dcz[drows, 2 * D + g * STEP:2 * D + (g + 1) * STEP]
            do4 = jnp.concatenate([do4 * m for m in ones], 0)
            q4 = s.dcz[drows, cols]
            q4 = jnp.concatenate([q4 * m for m in eighth], 0)
            dp = nt(do4, s.v[q, :, cols])
            pr = s.p[j, 3 * q + g]
            ds = (pr * (dp - jnp.sum(pr * dp, -1, keepdims=True))).astype(BF16)
            dq4 = nn(ds, s.k[q, :, cols])
            dq = sum(dq4[h * SEQ:(h + 1) * SEQ] * eighth32[h] for h in range(4))
            t.add(2 + 1, jnp.sum(dq, 0, keepdims=True), g * STEP)
            s.dcz[drows, cols] = dq.astype(BF16)
            s.dk[q, :, cols] = s.dk[q, :, cols] + tn(ds, q4)
            s.dv[q, :, cols] = s.dv[q, :, cols] + tn(pr.astype(BF16), do4)
            s.dcz[drows, D + g * STEP:D + (g + 1) * STEP] = s.dk[q, slot, cols].astype(BF16)
            dv = s.dv[q, slot, cols]
            s.dcz[drows, 2 * D + g * STEP:2 * D + (g + 1) * STEP] = dv.astype(BF16)
            t.add(2 + 2, jnp.sum(dv, 0, keepdims=True), g * STEP)
    s.post(1, Q, j)
    dc = s.dcz[rows, 0:3 * D]
    w.ready(j, 0)
    back = w.qkv.reshape(3 * D, D)
    da = jnp.concatenate([nn(dc, back[:, n:n + STEP]) for n in range(0, D, STEP)], 1)
    dx, dgain, dshift = norm_backward(da, p.gain(0), s.hat1.at[j], s.inv1.at[j])
    t.add(0, dgain)
    t.add(2, dshift)
    return dm1 + dx


def partner_copy(src, dst, sems):
    return pltpu.make_async_remote_copy(
        src_ref=src, dst_ref=dst, send_sem=sems.at[0], recv_sem=sems.at[1],
        device_id={"section": 1 - lax.axis_index("section")}, device_id_type=MESH)


def rank(axis):
    return lax.rem(lax.div(lax.axis_index("dp"), STRIDE[axis]), 4)


def main_kernel(tokens, out_grad, passes, embed, w_qkv, w_out, w_up, w_down, gains, biases, up_bias,
                keep, got, q_out, o_out, u_out, d_out, sums, sums_other, xs, turned,
                qkv_v, out_v, up_v, down_v, k, v, prob, hat1, inv1, hat2, inv2, slope, dk, dv, state,
                ao, b, e, dcz, df, dr, small, halves, leave, arrive, give, y0, entry,
                q2s, u2s, d2s, d3s, q2r, u2r, d2r, d3r,
                q4s, u4s, q4r, u4r, vec, vec_in,
                wsem, tsem, usem, xsem, hsem, gsem, psem, vsem, psend, precv, plocal, stage, esend, erecv,
                asend, arecv, ssend, srecv):
    sec = lax.axis_index("section")
    dp = lax.axis_index("dp")
    loads = [pltpu.make_async_copy(w_qkv.at[0, :, pl.ds(i * D, D)], qkv_v.at[i], wsem.at[i]) for i in range(3)]
    loads += [pltpu.make_async_copy(src.at[0], dst, wsem.at[3 + i]) for i, (src, dst) in enumerate(
        ((w_out, out_v), (w_up, up_v), (w_down, down_v)))]
    for c in loads:
        c.start()
    ranks = [rank(axis) for axis in AXES]
    peers = [[lax.rem(ranks[g] + by, 4) for by in range(4)] for g in range(3)]
    places = [[dp + (peers[g][by] - ranks[g]) * STRIDE[AXES[g]] for by in range(4)] for g in range(3)]
    offsets = [[pl.multiple_of(peers[g][by] * D, D) for by in range(4)] for g in range(3)]
    seconds = [lax.div(peers[Q][by], 3) for by in range(4)]
    barrier = pltpu.get_barrier_semaphore()
    for g in range(3):
        for by in (1, 2, 3):
            pl.semaphore_signal(barrier, inc=1, device_id={"dp": places[g][by]}, device_id_type=MESH)
            pl.semaphore_signal(barrier, inc=1, device_id={"dp": places[g][by], "section": 1 - sec},
                                device_id_type=MESH)
    planes = {}
    for g, axis in ((U, "y"), (Q, "z")):
        pos = rank(axis)
        planes[g] = [[places[g][by] + (lax.rem(pos + over, 4) - pos) * STRIDE[axis] for by in range(4)]
                     for over in range(4)]
        for over in (1, 2, 3):
            for by in (1, 2, 3):
                pl.semaphore_signal(barrier, inc=1, device_id={"dp": planes[g][over][by]}, device_id_type=MESH)
    pl.semaphore_signal(barrier, inc=1, device_id={"section": 1 - sec}, device_id_type=MESH)
    give[...] = jnp.where(sec == 0, out_grad[...], tokens[...])
    own = jnp.where(sec == 0, tokens[...], out_grad[...])
    pl.semaphore_wait(barrier, 37)
    exchange = partner_copy(give, halves.at[sec], xsem)
    exchange.start()
    halves[sec] = own

    wide = (dcz, df, e)

    def source(which, g, j, by):
        rows = pl.ds(pl.multiple_of(j * R, R), R)
        if g == Q:
            return ao.at[seconds[by], rows] if which == 0 else dcz.at[rows, pl.ds(offsets[g][by], D)]
        if g == U:
            return b.at[rows] if which == 0 else df.at[rows, pl.ds(offsets[g][by], D)]
        return e.at[rows, pl.ds(offsets[g][by], D)] if which == 0 else dr.at[rows]

    def target(which, g, j, by, first):
        if which == 0:
            return xs.at[g, j, peers[g][by]]
        if first:
            return y0.at[g, peers[g][by]]
        return wide[g].at[pl.ds(pl.multiple_of(j * R, R), R), pl.ds(offsets[g][by], D)]

    def remote(which, g, j, by, first):
        return pltpu.make_async_remote_copy(
            src_ref=source(which, g, j, by), dst_ref=target(which, g, j, 0, first),
            send_sem=psend.at[which, g, j, by], recv_sem=precv.at[which, g, j, ranks[g]],
            device_id={"dp": places[g][by], "section": sec if first else 1 - sec}, device_id_type=MESH)

    def inside(which, g):
        return pltpu.make_async_copy(source(which, g, 0, 0), target(which, g, 0, 0, True), plocal.at[which, g])

    def post(which, g, j):
        @pl.when(j == 0)
        def _():
            for by in (2, 1, 3):
                remote(which, g, 0, by, True).start()
            inside(which, g).start()

        @pl.when(j > 0)
        def _():
            for by in (2, 1, 3, 0):
                remote(which, g, j, by, False).start()

    def arrived(which, g, j, first=False):
        for by in range(1 if first else 0, 4):
            there = target(which, g, j, by, first)
            pltpu.make_async_remote_copy(
                src_ref=there, dst_ref=there, send_sem=psend.at[which, g, 0, 0],
                recv_sem=precv.at[which, g, j, peers[g][by]],
                device_id={"dp": places[g][1]}, device_id_type=MESH).wait_recv()
        if first:
            inside(which, g).wait()

    class Sum:
        def __init__(self, g, m, n):
            if g == Q:
                self.refs = [r.at[1 + m, :, pl.ds(n * STEP, STEP)] for r in (hat1, hat2)]
            else:
                at = 2 * (n + (3 if g == U else 0))
                self.refs = [slope.at[1 + m, :, pl.ds((at + h) * STEP, STEP)] for h in range(2)]

        def read(self):
            return jnp.concatenate([r[...] for r in self.refs], 0)

        def write(self, value):
            size = STEP // len(self.refs)
            for i, r in enumerate(self.refs):
                r[...] = value[i * size:(i + 1) * size]

    tiles = [(m, n) for m in range(3) for n in range(3)]
    stacks = {Q: q2s, U: u2s, W: d2s}
    second = {g: r.reshape(D, D) for g, r in stacks.items()}

    def turn(first):
        blocks = [(qkv_v.at[i], 0) for i in range(3)] + [(out_v, 0)]
        blocks += [(down_v.at[pl.ds(i * D, D)], 0) for i in range(4)] + [(up_v, i * D) for i in range(4)]
        copies = []
        for i, (src, lo) in enumerate(blocks):
            if first:
                for order in {0: (0,), 1: (1,), 2: (2,), 3: (3,), 4: (5,), 8: (4,)}.get(i, ()):
                    loads[order].wait()
            if i >= 3:
                copies[i - 3].wait()
            dst = second[i % 3]
            def flip(m, carry):
                at = pl.multiple_of(m * STEP, STEP)
                for n in range(3):
                    dst[n * STEP:(n + 1) * STEP, pl.ds(at, STEP)] = src[
                        pl.ds(at, STEP), lo + n * STEP:lo + (n + 1) * STEP].T
                return carry
            lax.fori_loop(0, 3, flip, 0)
            copies.append(pltpu.make_async_copy(dst, turned.at[i], tsem.at[i]))
            copies[-1].start()
        for c in copies[-3:]:
            c.wait()

    returns = [[pltpu.make_async_copy(turned.at[pl.ds(0, 3)], qkv_v, usem.at[0])],
               [pltpu.make_async_copy(turned.at[3], out_v, usem.at[1])],
               [pltpu.make_async_copy(turned.at[4 + i], up_v.at[:, pl.ds(i * D, D)], usem.at[2 + i])
                for i in range(4)],
               [pltpu.make_async_copy(turned.at[8 + i], down_v.at[pl.ds(i * D, D)], usem.at[6 + i])
                for i in range(4)]]

    w = Names(qkv=qkv_v, out=out_v, up=up_v, down=down_v)

    def wait(j, i):
        @pl.when((j == 0) & (sec == 0))
        def _():
            loads[i].wait()

    def done(j, i):
        @pl.when(j == SLOTS - 1)
        def _():
            for c in returns[i]:
                c.start()

    def ready(j, i):
        @pl.when(j == SLOTS - 1)
        def _():
            for c in returns[i]:
                c.wait()
    w.wait, w.done, w.ready = wait, done, ready
    p = Names(gain=lambda i: gains[0, i:i + 1, :], bias=lambda i: biases[i],
              up=lambda lo, hi: up_bias[:, lo:hi])
    s = Names(k=k, v=v, p=prob, hat1=hat1, inv1=inv1, hat2=hat2, inv2=inv2, slope=slope, dk=dk, dv=dv,
              ao=ao, b=b, e=e, dcz=dcz, df=df, dr=dr, post=post)
    small[...] = jnp.zeros_like(small)

    def add(i, value, at=0):
        cols = slice(at, at + value.shape[1])
        small[i:i + 1, cols] = small[i:i + 1, cols] + value
    t = Names(add=add)
    k[...] = jnp.zeros_like(k)
    v[...] = jnp.zeros_like(v)
    dk[...] = jnp.zeros_like(dk)
    dv[...] = jnp.zeros_like(dv)
    row = lax.broadcasted_iota(jnp.int32, (R, 1), 0)
    count = jnp.where(row < SEQ, passes[0], passes[1]) - 1
    count = jnp.where(sec == 0, SLOTS, count)
    hand = partner_copy(leave, arrive, hsem)
    present = partner_copy(give, got, gsem)
    partial = [partner_copy(r, r, psem.at[i]) for i, r in enumerate((q2s, u2s, d2s))]

    def joined():
        return jnp.concatenate([halves[h, i] for i in range(2) for h in range(2)], 0).astype(F32)

    slots = jnp.where(sec == 0, 1, SLOTS)

    def step_forward(j, carry):
        h = state[...]
        r = forward(j, h + embed[pl.ds(j + sec, 1), :], w, p, s)
        state[...] = jnp.where(count > j, r, h)
        return carry

    def step_backward(i, carry):
        j = slots - 1 - i
        g = state[...]
        du = backward(j, jnp.where(count > j, g, 0.0), w, p, s, t)
        entry[j] = jnp.sum(du, 0, keepdims=True)
        state[...] = jnp.where(count > j, du, g)
        return carry

    @pl.when(sec == 0)
    def _():
        exchange.wait()
        state[...] = joined()

    @pl.when(sec == 1)
    def _():
        turn(True)
        exchange.wait()
        hand.wait_recv()
        state[...] = arrive[...].astype(F32)

    lax.fori_loop(0, slots, step_forward, 0)

    @pl.when(sec == 0)
    def _():
        leave[...] = state[...].astype(BF16)
        hand.start()
        turn(False)
        for group in returns:
            for c in group:
                c.start()

        def staging(g, j):
            return [pltpu.make_async_copy(xs.at[g, j, i], second[g].at[pl.ds(i * R, R)], stage.at[g, i])
                    for i in range(4)]

        def bring(g, j):
            arrived(0, g, j)
            for c in staging(g, j):
                c.start()

        def clear(m, carry):
            for g in range(3):
                for n in range(3):
                    Sum(g, m, n).write(jnp.zeros((STEP, STEP), F32))
            return carry
        lax.fori_loop(0, 3, clear, 0)
        for g in (W, U, Q):
            bring(g, SLOTS - 1)
        for group in returns:
            for c in group:
                c.wait()

        def gather(i, carry):
            j = SLOTS - 1 - i
            rows = pl.ds(pl.multiple_of(j * R, R), R)
            for g in (W, U, Q):
                for c in staging(g, j):
                    c.wait()
                arrived(1, g, j)

                def across(m, carry):
                    left = second[g][0:ROWS, pl.ds(pl.multiple_of(m * STEP, STEP), STEP)]
                    for n in range(3):
                        right = jnp.concatenate([
                            wide[g][rows, x * D + n * STEP:x * D + (n + 1) * STEP] for x in range(4)], 0)
                        held = Sum(g, m, n)
                        held.write(held.read() + tn(left, right))
                    return carry
                lax.fori_loop(0, 3, across, 0)

                @pl.when(j > 1)
                def _():
                    bring(g, j - 1)

                @pl.when(j == 1)
                def _():
                    def rounded(m, carry):
                        there = pl.ds(pl.multiple_of(m * STEP, STEP), STEP)
                        for n in range(3):
                            second[g][there, n * STEP:(n + 1) * STEP] = Sum(g, m, n).read().astype(BF16)
                        return carry
                    lax.fori_loop(0, 3, rounded, 0)
                    partial[g].start()
            return carry
        lax.fori_loop(0, SLOTS - 1, gather, 0)
        hand.wait()
        state[...] = arrive[...].astype(F32)

    @pl.when(sec == 1)
    def _():
        final = state[...].astype(BF16)
        for i in range(2):
            give[i] = final[i * SEQ:i * SEQ + 32]
            keep[i] = final[i * SEQ + 32:i * SEQ + 64]
        present.start()
        state[...] = joined()

    lax.fori_loop(0, slots, step_backward, 0)
    fetched = [[pltpu.make_async_copy(xs.at[g, 0, i], up_v.at[pl.ds(i * R, R), pl.ds(g * D, D)], stage.at[g, i])
                for i in range(4)] for g in range(3)]
    for g in (W, U, Q):
        arrived(0, g, 0, True)
        for c in fetched[g]:
            c.start()

    @pl.when(sec == 0)
    def _():
        final = state[...].astype(BF16)
        for i in range(2):
            keep[i] = final[i * SEQ:i * SEQ + 32]
            give[i] = final[i * SEQ + 32:i * SEQ + 64]
        present.start()
        for g in range(3):
            partial[g].wait_send()

    @pl.when(sec == 1)
    def _():
        leave[...] = state[...].astype(BF16)
        hand.start()

    def shares(axis, number):
        pos = rank(axis)
        copies = []
        for by in (1, 2, 3):
            there = dp + (lax.rem(pos + by, 4) - pos) * STRIDE[axis]
            copies.append(pltpu.make_async_remote_copy(
                src_ref=vec.at[number], dst_ref=vec_in.at[number, by - 1], send_sem=ssend.at[number, by - 1],
                recv_sem=srecv.at[number, by - 1], device_id={"dp": there}, device_id_type=MESH))
        return copies
    shared = [shares(axis, number) for number, axis in enumerate(("z", "y", "x"))]

    def share_start(number):
        for c in shared[number]:
            c.start()

    def share_next(number):
        for c in shared[number]:
            c.wait_recv()
        vec[number + 1] = vec[number] + vec_in[number, 0] + vec_in[number, 1] + vec_in[number, 2]
        if number < 2:
            share_start(number + 1)
    vec[0] = small[...]
    for j in range(SLOTS):
        vec[0, 8 + j:9 + j, :] = entry[j]
    share_start(0)

    class Part:
        def __init__(self, axis, number, block, landing):
            self.axis, self.number, self.block, self.landing = axis, number, block, landing
            self.pos = rank(axis)

        def copies(self, c):
            made = []
            for by in (2, 1, 3):
                to = lax.rem(self.pos + by, 4)
                made.append(pltpu.make_async_remote_copy(
                    src_ref=self.block(to, columns(c)), dst_ref=self.landing(by - 1, columns(c)),
                    send_sem=esend.at[self.number, c, by - 1], recv_sem=erecv.at[self.number, c, by - 1],
                    device_id={"dp": dp + (to - self.pos) * STRIDE[self.axis]}, device_id_type=MESH))
            return made

        def start(self, c):
            for copy in self.copies(c):
                copy.start()

        def finish(self, c, store):
            for copy in self.copies(c):
                copy.wait_recv()
            own = self.block(self.pos, columns(c))
            others = [self.landing(i, columns(c)) for i in range(3)]
            for i in range(4 if len(own.shape) == 3 else 1):
                key = (i,) if len(own.shape) == 3 else (slice(None),)
                value = own[key].astype(F32)
                for other in others:
                    value = value + other[key].astype(F32)
                store(i, columns(c), value)

        def drain(self, c):
            for copy in self.copies(c):
                copy.wait_send()

    def columns(c):
        return pl.ds(pl.multiple_of(c * STEP, STEP), STEP)

    d2 = Part("z", 0, lambda i, c: d2s.at[:, i, :, c], lambda i, c: d2r.at[i, :, :, c])
    u2 = Part("x", 1, lambda i, c: u2s.at[:, i, :, c], lambda i, c: u2r.at[i, :, :, c])
    q2 = Part("y", 2, lambda i, c: q2s.at[i, :, c], lambda i, c: q2r.at[i, :, c])
    d3 = Part("x", 3, lambda i, c: d3s.at[i, :, c], lambda i, c: d3r.at[i, :, c])

    def each(body):
        def step(c, carry):
            body(c)
            return carry
        lax.fori_loop(0, 3, step, 0)

    def multiply(g, one):
        for c in fetched[g]:
            c.wait()
        arrived(1, g, 0, True)

        @pl.when(sec == 1)
        def _():
            partial[g].wait_recv()

        def across(c):
            right = y0[g, :, :, columns(c)].reshape(ROWS, STEP)
            for m in range(3):
                part = second[g].at[m * STEP:(m + 1) * STEP, columns(c)]
                held = jnp.where(sec == 1, part[...].astype(F32), 0.0)
                left = up_v[0:ROWS, g * D + m * STEP:g * D + (m + 1) * STEP]
                part[...] = (held + tn(left, right)).astype(BF16)
            one.start(c)
        each(across)

    def to_rows(dst):
        def store(i, at, value):
            dst[i, :, at] = value.astype(BF16)
        return store

    def twelve(rows):
        return jnp.concatenate([rows, jnp.zeros((4, STEP), F32)], 0).astype(BF16)

    def to_plane_u(y, at, value):
        for z in range(4):
            u4s[y, z, :, at] = twelve(value[12 * z:12 * z + 12])

    def to_plane_q(i, at, value):
        for x in range(4):
            for z in range(4):
                q4s[z, x, :, at] = twelve(value[48 * x + 12 * z:48 * x + 12 * z + 12])

    def to_out(i, at, value):
        d_out[:, at] = value

    def plane(g, src, dst):
        axis = "y" if g == U else "z"
        pos = rank(axis)
        return [pltpu.make_async_remote_copy(
            src_ref=src.at[lax.rem(pos + over, 4), peers[g][by]], dst_ref=dst.at[over, ranks[g]],
            send_sem=asend.at[g, over, by], recv_sem=arecv.at[g, over, ranks[g]],
            device_id={"dp": planes[g][over][by]}, device_id_type=MESH)
            for over in range(4) for by in range(4) if over or by]

    def plane_sum(g, dst, r):
        value = dst[0, r].astype(F32)
        for over in (1, 2, 3):
            value = value + dst[over, r].astype(F32)
        return value[0:12]

    def plane_arrived(g, dst):
        for over in range(4):
            for by in range(4):
                if over or by:
                    there = dst.at[over, peers[g][by]]
                    pltpu.make_async_remote_copy(
                        src_ref=there, dst_ref=there, send_sem=asend.at[g, 0, 0],
                        recv_sem=arecv.at[g, over, peers[g][by]],
                        device_id={"dp": places[g][1]}, device_id_type=MESH).wait_recv()

    multiply(W, d2)
    multiply(U, u2)
    multiply(Q, q2)
    share_next(0)

    for which in range(2):
        for g in range(3):
            for by in (1, 2, 3):
                remote(which, g, 0, by, True).wait_send()

    @pl.when(sec == 1)
    def _():
        hand.wait_send()

        def drain(j, carry):
            for which in range(2):
                for g in range(3):
                    for by in range(4):
                        remote(which, g, j, by, False).wait_send()
            return carry
        lax.fori_loop(1, SLOTS, drain, 0)
    present.wait()

    def second_done(c):
        u2.finish(c, to_plane_u)
        d2.finish(c, to_rows(d3s))
        d3.start(c)
    each(second_done)
    spread_u = plane(U, u4s, u4r)
    for copy in spread_u:
        copy.start()
    u4r[0, ranks[U]] = u4s[rank("y"), ranks[U]]
    each(lambda c: q2.finish(c, to_plane_q))
    spread_q = plane(Q, q4s, q4r)
    for copy in spread_q:
        copy.start()
    q4r[0, ranks[Q]] = q4s[rank("z"), ranks[Q]]
    share_next(1)

    def drained(c):
        for one in (d2, u2, q2):
            one.drain(c)
    each(drained)
    each(lambda c: d3.finish(c, to_out))
    share_next(2)
    sums[...] = vec[3]
    other = partner_copy(vec.at[3], sums_other, vsem)
    other.start()
    plane_arrived(U, u4r)
    for i in range(4):
        u_out[:, i * D:(i + 1) * D] = plane_sum(U, u4r, i)
    plane_arrived(Q, q4r)
    for i in range(3):
        q_out[:, i * D:(i + 1) * D] = plane_sum(Q, q4r, i)
    o_out[...] = plane_sum(Q, q4r, 3)
    each(lambda c: d3.drain(c))
    for copies in shared + [spread_u, spread_q]:
        for copy in copies:
            copy.wait_send()
    other.wait()


def main(*args):
    vmem = pl.BlockSpec(memory_space=VM)
    hbm = pl.BlockSpec(memory_space=pltpu.HBM)
    dma = pltpu.SemaphoreType.DMA
    return pl.pallas_call(
        main_kernel,
        out_shape=[jax.ShapeDtypeStruct(dims, dtype) for dims, dtype in (
            ((2, 32, D), BF16), ((2, 32, D), BF16), ((12, 3 * D), F32), ((12, D), F32), ((12, FF), F32), ((48, D), F32),
            ((16, D), F32), ((16, D), F32), ((3, SLOTS, 4, R, D), BF16), ((12, D, D), BF16))],
        in_specs=[vmem, vmem, pl.BlockSpec(memory_space=pltpu.SMEM), vmem] + [hbm] * 4 + [vmem] * 3,
        out_specs=[vmem] * 8 + [hbm] * 2,
        scratch_shapes=[
            VM((3, D, D), BF16), VM((D, D), BF16), VM((D, FF), BF16), VM((FF, D), BF16),
            VM((2, 256, D), BF16), VM((2, 256, D), BF16), VM((SLOTS, 6, 256, 256), F32),
            VM((SLOTS, R, D), F32), VM((SLOTS, R, 128), F32), VM((SLOTS, R, D), F32), VM((SLOTS, R, 128), F32),
            VM((SLOTS, R, FF), F32), VM((2, 256, D), F32), VM((2, 256, D), F32), VM((R, D), F32),
            VM((2, ROWS, D), BF16), VM((ROWS, D), BF16), VM((ROWS, FF), BF16), VM((ROWS, 4 * D), BF16),
            VM((ROWS, FF), BF16), VM((ROWS, D), BF16), VM((16, D), F32),
            VM((2, 2, 32, D), BF16), VM((R, D), BF16), VM((R, D), BF16), VM((2, 32, D), BF16),
            VM((3, 4, R, D), BF16), VM((SLOTS, 1, D), F32),
            VM((4, 192, D), BF16), VM((4, 4, 48, D), BF16), VM((4, 4, 48, D), BF16),
            VM((4, 48, D), BF16),
            VM((3, 192, D), BF16), VM((3, 4, 48, D), BF16), VM((3, 4, 48, D), BF16),
            VM((3, 48, D), BF16)]
        + [VM((4, 4, 16, D), BF16)] * 4 + [VM((4, 16, D), F32), VM((3, 3, 16, D), F32)]
        + [dma((6,)), dma((12,)), dma((10,)), dma((2,)), dma((2,)), dma((2,)), dma((3, 2)), dma((2,)),
           dma((2, 3, SLOTS, 4)), dma((2, 3, SLOTS, 4)), dma((2, 3)), dma((3, 4)), dma((4, 3, 3)), dma((4, 3, 3)),
           dma((2, 4, 4)), dma((2, 4, 4)), dma((3, 3)), dma((3, 3))],
        compiler_params=pltpu.CompilerParams(collective_id=0, has_side_effects=True, vmem_limit_bytes=int(63.4 * 2**20)),
        name="layers",
    )(*args)


def finish_kernel(keep, got, q_in, o_in, u_in, d_in, sums, other,
                  hidden, token, q_out, o_out, u_out, d_out, g_gains, g_bias, g_up, g_embed):
    sec = lax.axis_index("section")
    dp = lax.axis_index("dp")
    hidden[...] = jnp.where(sec == 0, got[...], keep[...])
    token[...] = jnp.where(sec == 0, keep[...], got[...])
    for i in range(12):
        q_out[i] = q_in[i:i + 1, :]
        o_out[i] = o_in[i:i + 1, :]
        u_out[i] = u_in[i:i + 1, :]
    d_out[0] = d_in[...]
    turned = pltpu.roll(sums[...], lax.rem(D - dp * 12, D), 1)
    g_gains[0] = turned[0:2, 0:12]
    for i in range(6):
        g_bias[i] = turned[2 + i:3 + i, 0:12]
    lines = sums[12:13, :]
    for i in range(1, 4):
        lines = jnp.where(lax.div(dp, 16) == i, sums[12 + i:13 + i, :], lines)
    g_up[...] = pltpu.roll(lines, lax.rem(D - lax.rem(dp, 16) * 48, D), 1)[:, 0:48]
    mine, theirs = sums[8:12, :], other[8:12, :]
    rows = jnp.concatenate([jnp.where(sec == 0, mine, theirs)[0:1], jnp.where(sec == 0, theirs, mine)], 0)
    g_embed[...] = pltpu.roll(rows, lax.rem(D - (sec * 64 + dp) * 6, D), 1)[:, 0:6]


def finish(*args):
    vmem = pl.BlockSpec(memory_space=VM)
    return pl.pallas_call(
        finish_kernel,
        out_shape=[jax.ShapeDtypeStruct(dims, dtype) for dims, dtype in (
            ((2, 32, D), BF16), ((2, 32, D), BF16), ((12, 1, 3 * D), F32), ((12, 1, D), F32), ((12, 1, FF), F32),
            ((1, 48, D), F32), ((1, 2, 12), F32), ((6, 1, 12), F32), ((1, 48), F32), ((5, 6), F32))],
        in_specs=[vmem] * 8, out_specs=[vmem] * 10,
        name="finish",
    )(*args)


def local(*args):
    args = list(args)
    args[9] = jnp.swapaxes(args[9], 0, 1)
    outs = list(finish(*main(*args)[:8]))
    for i in (2, 3, 4, 7):
        outs[i] = jnp.swapaxes(outs[i], 0, 1)
    return tuple(outs)


def solution(mesh):
    split = ("section",)
    placed = (
        P("dp", "section", None), P("dp", "section", None), P("dp"), P(),
        P("section", None, None), P("section", None, None), P("section", None, None), P("section", None, None),
        P("section", None, None), P("section", None, None), P("section", None))
    return jax.shard_map(
        local, mesh=mesh, in_specs=placed,
        out_specs=(
            P("dp", "section", None), P("dp", "section", None),
            P("section", "dp", None), P("section", "dp", None), P("section", "dp", None), P("section", "dp", None),
            P("section", None, "dp"), P("section", None, "dp"), P("section", "dp"), P(None, ("section", "dp"))),
        check_vma=False)
```

profile of v0, /device:TPU:1, one launch (start us, length us, event | category | flops | bytes accessed | tf_op | source)
XLA Modules:
  0.0 111.1 jit_solution(16416489005164545709)
XLA Ops:
  0.6 108.2 %layers.1 = (bf16[2,32,768]{2,1,0:T(8,128)(2,1)}, bf16[2,32,768]{2,1,0:T(8,128)(2,1)}, f32[12,2304]{1,0:T(8,128)}, f32[12,768]{1,0:T(8,128)}, f32[12,3072]{1,0:T...) custom-call(bf16[2,32,768]{2,1,0:T(8,128)(2,1)} %tokens.1, ...), custom_call_target="tpu_custom_call" | custom-call | tf_op jit(solution)/shard_map/layers/pallas_call | solution.py:731
  108.8 2.1 %finish.1 = (bf16[2,32,768]{2,1,0:T(8,128)(2,1)}, bf16[2,32,768]{2,1,0:T(8,128)(2,1)}, f32[12,1,2304]{2,1,0:T(1,128)}, f32[12,1,768]{2,1,0:T(1,128)}, f32[12,1,3...) custom-call(bf16[2,32,768]{2,1,0:T(8,128)(2,1)} %get-tuple-element.2, ...), custom_call_target="tpu_custom_call" | custom-call | tf_op jit(solution)/shard_map/finish/pallas_call | solution.py:786
where the time goes:
time: 111 us
  Pallas kernels  110 us (99%)
    pallas_call x1, Pallas kernels, main(): pl.pallas_call(main_kernel, out_shape=[jax.ShapeDtypeStruct(dims, dtype)...  108 us

commit v1 on v0

--- a/solution.py
+++ b/solution.py
@@ -96,22 +96,21 @@
     w.done(j, 0)
     ones = lane_masks(1.0, F32)
     eighth = lane_masks(0.125, BF16)
-    col = lax.broadcasted_iota(jnp.int32, (SEQ, KEYS), 1)
-    row = lax.broadcasted_iota(jnp.int32, (SEQ, KEYS), 0)
-    allow = ((col & 63) <= row) & (col < (j + 1) * SEQ)
+    key = lax.broadcasted_iota(jnp.int32, (KEYS, STEP), 0)
+    place = lax.broadcasted_iota(jnp.int32, (KEYS, STEP), 1) & 63
+    allow = ((key & 63) <= place) & (key < (j + 1) * SEQ)
     veto = jnp.where(allow, 0.0, -1e30)
-    veto = jnp.concatenate([veto] * 4, 0)
     for q in range(2):
         qrows = pl.ds(pl.multiple_of(j * R + q * SEQ, SEQ), SEQ)
         for g in range(3):
             cols = slice(g * STEP, (g + 1) * STEP)
             q4 = s.dcz[qrows, cols]
             q4 = jnp.concatenate([q4 * m for m in eighth], 0)
-            sc = nt(q4, s.k[q, :, cols]) + veto
-            ex = jnp.exp(sc - jnp.max(sc, -1, keepdims=True))
-            pr = ex * (1.0 / jnp.sum(ex, -1, keepdims=True))
+            sc = nt(s.k[q, :, cols], q4) + veto
+            ex = jnp.exp(sc - jnp.max(sc, 0, keepdims=True))
+            pr = ex * (1.0 / jnp.sum(ex, 0, keepdims=True))
             s.p[j, 3 * q + g] = pr
-            o4 = nn(pr.astype(BF16), s.v[q, :, cols])
+            o4 = tn(pr.astype(BF16), s.v[q, :, cols])
             o = sum(o4[h * SEQ:(h + 1) * SEQ] * ones[h] for h in range(4))
             s.ao[1, qrows, cols] = o.astype(BF16)
     s.post(0, Q, j)
@@ -125,12 +124,11 @@
     w.wait(j, 4)
     for n in range(0, FF, STEP):
         f = nn(b, w.up[:, n:n + STEP]) + p.up(n, n + STEP)
-        ff = f * f
-        half = 0.5 + 0.5 * jnp.tanh(f * (0.7978845608 + (0.7978845608 * 0.044715) * ff))
-        e = f * half
-        s.e[rows, n:n + STEP] = e.astype(BF16)
-        s.slope[j, :, n:n + STEP] = half + e * (1.0 - half) * (
-            2 * 0.7978845608 + (6 * 0.7978845608 * 0.044715) * ff)
+        t = jnp.tanh(0.7978845608 * (f + 0.044715 * f * f * f))
+        half = 0.5 * (1.0 + t)
+        s.e[rows, n:n + STEP] = (f * half).astype(BF16)
+        s.slope[j, :, n:n + STEP] = half + 0.5 * f * (1.0 - t * t) * (
+            0.7978845608 + 0.7978845608 * 3 * 0.044715 * f * f)
     w.done(j, 2)
     s.post(0, W, j)
     e = s.e[rows]
@@ -178,15 +176,15 @@
             do4 = jnp.concatenate([do4 * m for m in ones], 0)
             q4 = s.dcz[drows, cols]
             q4 = jnp.concatenate([q4 * m for m in eighth], 0)
-            dp = nt(do4, s.v[q, :, cols])
+            dp = nt(s.v[q, :, cols], do4)
             pr = s.p[j, 3 * q + g]
-            ds = (pr * (dp - jnp.sum(pr * dp, -1, keepdims=True))).astype(BF16)
-            dq4 = nn(ds, s.k[q, :, cols])
+            ds = (pr * (dp - jnp.sum(pr * dp, 0, keepdims=True))).astype(BF16)
+            dq4 = tn(ds, s.k[q, :, cols])
             dq = sum(dq4[h * SEQ:(h + 1) * SEQ] * eighth32[h] for h in range(4))
             t.add(2 + 1, jnp.sum(dq, 0, keepdims=True), g * STEP)
             s.dcz[drows, cols] = dq.astype(BF16)
-            s.dk[q, :, cols] = s.dk[q, :, cols] + tn(ds, q4)
-            s.dv[q, :, cols] = s.dv[q, :, cols] + tn(pr.astype(BF16), do4)
+            s.dk[q, :, cols] = s.dk[q, :, cols] + nn(ds, q4)
+            s.dv[q, :, cols] = s.dv[q, :, cols] + nn(pr.astype(BF16), do4)
             s.dcz[drows, D + g * STEP:D + (g + 1) * STEP] = s.dk[q, slot, cols].astype(BF16)
             dv = s.dv[q, slot, cols]
             s.dcz[drows, 2 * D + g * STEP:2 * D + (g + 1) * STEP] = dv.astype(BF16)
@@ -215,10 +213,10 @@
 def main_kernel(tokens, out_grad, passes, embed, w_qkv, w_out, w_up, w_down, gains, biases, up_bias,
                 keep, got, q_out, o_out, u_out, d_out, sums, sums_other, xs, turned,
                 qkv_v, out_v, up_v, down_v, k, v, prob, hat1, inv1, hat2, inv2, slope, dk, dv, state,
-                ao, b, e, dcz, df, dr, small, halves, leave, arrive, give, y0, entry,
+                ao, b, e, dcz, df, dr, small, halves, leave, arrive, give, entry,
                 q2s, u2s, d2s, d3s, q2r, u2r, d2r, d3r,
                 q4s, u4s, q4r, u4r, vec, vec_in,
-                wsem, tsem, usem, xsem, hsem, gsem, psem, vsem, psend, precv, plocal, stage, esend, erecv,
+                wsem, tsem, usem, xsem, hsem, gsem, psem, vsem, psend, precv, stage, esend, erecv,
                 asend, arecv, ssend, srecv):
     sec = lax.axis_index("section")
     dp = lax.axis_index("dp")
@@ -264,43 +262,40 @@
             return b.at[rows] if which == 0 else df.at[rows, pl.ds(offsets[g][by], D)]
         return e.at[rows, pl.ds(offsets[g][by], D)] if which == 0 else dr.at[rows]
 
-    def target(which, g, j, by, first):
+    def slot_of(j):
+        return jnp.where(j == 0, SLOTS, j)
+
+    def landing(which, g, j, at, spare=False):
         if which == 0:
-            return xs.at[g, j, peers[g][by]]
-        if first:
-            return y0.at[g, peers[g][by]]
-        return wide[g].at[pl.ds(pl.multiple_of(j * R, R), R), pl.ds(offsets[g][by], D)]
-
-    def remote(which, g, j, by, first):
+            return xs.at[g, slot_of(j) if spare else j, at]
+        rows = pl.ds(pl.multiple_of(slot_of(j) * R, R), R)
+        return wide[g].at[rows, pl.ds(pl.multiple_of(at * D, D), D)]
+
+    def remote(which, g, j, by):
+        place, mark, at = places[g][by], ranks[g], ranks[g]
+        if by == 0:
+            place = jnp.where(j == 0, places[g][1], dp)
+            mark = jnp.where(j == 0, peers[g][1], ranks[g])
+            at = ranks[g] if which == 0 else mark
         return pltpu.make_async_remote_copy(
-            src_ref=source(which, g, j, by), dst_ref=target(which, g, j, 0, first),
-            send_sem=psend.at[which, g, j, by], recv_sem=precv.at[which, g, j, ranks[g]],
-            device_id={"dp": places[g][by], "section": sec if first else 1 - sec}, device_id_type=MESH)
-
-    def inside(which, g):
-        return pltpu.make_async_copy(source(which, g, 0, 0), target(which, g, 0, 0, True), plocal.at[which, g])
+            src_ref=source(which, g, j, by), dst_ref=landing(which, g, j, at, by == 0),
+            send_sem=psend.at[which, g, j, by], recv_sem=precv.at[which, g, j, mark],
+            device_id={"dp": place, "section": jnp.where(j == 0, sec, 1 - sec)}, device_id_type=MESH)
 
     def post(which, g, j):
-        @pl.when(j == 0)
-        def _():
-            for by in (2, 1, 3):
-                remote(which, g, 0, by, True).start()
-            inside(which, g).start()
-
-        @pl.when(j > 0)
-        def _():
-            for by in (2, 1, 3, 0):
-                remote(which, g, j, by, False).start()
-
-    def arrived(which, g, j, first=False):
-        for by in range(1 if first else 0, 4):
-            there = target(which, g, j, by, first)
+        for by in (2, 1, 3, 0):
+            remote(which, g, j, by).start()
+
+    def arrived(which, g, j):
+        for by in range(4):
+            at = peers[g][by]
+            if by == 0 and which == 0:
+                at = jnp.where(j == 0, peers[g][3], ranks[g])
+            there = landing(which, g, j, at, by == 0)
             pltpu.make_async_remote_copy(
                 src_ref=there, dst_ref=there, send_sem=psend.at[which, g, 0, 0],
                 recv_sem=precv.at[which, g, j, peers[g][by]],
                 device_id={"dp": places[g][1]}, device_id_type=MESH).wait_recv()
-        if first:
-            inside(which, g).wait()
 
     class Sum:
         def __init__(self, g, m, n):
@@ -355,21 +350,27 @@
     w = Names(qkv=qkv_v, out=out_v, up=up_v, down=down_v)
 
     def wait(j, i):
-        @pl.when((j == 0) & (sec == 0))
-        def _():
-            loads[i].wait()
+        if i == 3:
+            @pl.when((j == 0) & (sec == 0))
+            def _():
+                for c in loads[3:]:
+                    c.wait()
 
     def done(j, i):
-        @pl.when(j == SLOTS - 1)
-        def _():
-            for c in returns[i]:
-                c.start()
+        if i == 2:
+            @pl.when(j == SLOTS - 1)
+            def _():
+                for group in (returns[2], returns[1], returns[0]):
+                    for c in group:
+                        c.start()
 
     def ready(j, i):
-        @pl.when(j == SLOTS - 1)
-        def _():
-            for c in returns[i]:
-                c.wait()
+        if i == 3:
+            @pl.when(j == SLOTS - 1)
+            def _():
+                for group in (returns[3], returns[1], returns[0]):
+                    for c in group:
+                        c.wait()
     w.wait, w.done, w.ready = wait, done, ready
     p = Names(gain=lambda i: gains[0, i:i + 1, :], bias=lambda i: biases[i],
               up=lambda lo, hi: up_bias[:, lo:hi])
@@ -415,6 +416,8 @@
     def _():
         exchange.wait()
         state[...] = joined()
+        for c in loads[:3]:
+            c.wait()
 
     @pl.when(sec == 1)
     def _():
@@ -493,18 +496,23 @@
 
     @pl.when(sec == 1)
     def _():
+        for c in returns[3]:
+            c.start()
         final = state[...].astype(BF16)
         for i in range(2):
             give[i] = final[i * SEQ:i * SEQ + 32]
             keep[i] = final[i * SEQ + 32:i * SEQ + 64]
         present.start()
         state[...] = joined()
+        for c in returns[2]:
+            c.wait()
 
     lax.fori_loop(0, slots, step_backward, 0)
-    fetched = [[pltpu.make_async_copy(xs.at[g, 0, i], up_v.at[pl.ds(i * R, R), pl.ds(g * D, D)], stage.at[g, i])
-                for i in range(4)] for g in range(3)]
+    fetched = [[pltpu.make_async_copy(
+        xs.at[g, 0, peers[g][by]] if by else source(0, g, 0, 0),
+        up_v.at[pl.ds(by * R, R), pl.ds(g * D, D)], stage.at[g, by]) for by in range(4)] for g in range(3)]
     for g in (W, U, Q):
-        arrived(0, g, 0, True)
+        arrived(0, g, 0)
         for c in fetched[g]:
             c.start()
 
@@ -598,17 +606,24 @@
             return carry
         lax.fori_loop(0, 3, step, 0)
 
+    def shifted(lo, c):
+        return pl.ds(pl.multiple_of(lo + c * STEP, STEP), STEP)
+
     def multiply(g, one):
         for c in fetched[g]:
             c.wait()
-        arrived(1, g, 0, True)
+        arrived(1, g, 0)
 
         @pl.when(sec == 1)
         def _():
             partial[g].wait_recv()
 
         def across(c):
-            right = y0[g, :, :, columns(c)].reshape(ROWS, STEP)
+            spare = slice(SLOTS * R, (SLOTS + 1) * R)
+            own = dr if g == W else wide[g]
+            parts = [own[0:R, columns(c) if g == W else shifted(offsets[g][0], c)]]
+            parts += [wide[g][spare, shifted(offsets[g][by], c)] for by in (1, 2, 3)]
+            right = jnp.concatenate(parts, 0)
             for m in range(3):
                 part = second[g].at[m * STEP:(m + 1) * STEP, columns(c)]
                 held = jnp.where(sec == 1, part[...].astype(F32), 0.0)
@@ -669,8 +684,8 @@
 
     for which in range(2):
         for g in range(3):
-            for by in (1, 2, 3):
-                remote(which, g, 0, by, True).wait_send()
+            for by in range(4):
+                remote(which, g, 0, by).wait_send()
 
     @pl.when(sec == 1)
     def _():
@@ -680,7 +695,7 @@
             for which in range(2):
                 for g in range(3):
                     for by in range(4):
-                        remote(which, g, j, by, False).wait_send()
+                        remote(which, g, j, by).wait_send()
             return carry
         lax.fori_loop(1, SLOTS, drain, 0)
     present.wait()
@@ -732,7 +747,7 @@
         main_kernel,
         out_shape=[jax.ShapeDtypeStruct(dims, dtype) for dims, dtype in (
             ((2, 32, D), BF16), ((2, 32, D), BF16), ((12, 3 * D), F32), ((12, D), F32), ((12, FF), F32), ((48, D), F32),
-            ((16, D), F32), ((16, D), F32), ((3, SLOTS, 4, R, D), BF16), ((12, D, D), BF16))],
+            ((16, D), F32), ((16, D), F32), ((3, SLOTS + 1, 4, R, D), BF16), ((12, D, D), BF16))],
         in_specs=[vmem, vmem, pl.BlockSpec(memory_space=pltpu.SMEM), vmem] + [hbm] * 4 + [vmem] * 3,
         out_specs=[vmem] * 8 + [hbm] * 2,
         scratch_shapes=[
@@ -740,17 +755,17 @@
             VM((2, 256, D), BF16), VM((2, 256, D), BF16), VM((SLOTS, 6, 256, 256), F32),
             VM((SLOTS, R, D), F32), VM((SLOTS, R, 128), F32), VM((SLOTS, R, D), F32), VM((SLOTS, R, 128), F32),
             VM((SLOTS, R, FF), F32), VM((2, 256, D), F32), VM((2, 256, D), F32), VM((R, D), F32),
-            VM((2, ROWS, D), BF16), VM((ROWS, D), BF16), VM((ROWS, FF), BF16), VM((ROWS, 4 * D), BF16),
-            VM((ROWS, FF), BF16), VM((ROWS, D), BF16), VM((16, D), F32),
+            VM((2, ROWS, D), BF16), VM((ROWS, D), BF16), VM((ROWS + R, FF), BF16), VM((ROWS + R, 4 * D), BF16),
+            VM((ROWS + R, FF), BF16), VM((ROWS, D), BF16), VM((16, D), F32),
             VM((2, 2, 32, D), BF16), VM((R, D), BF16), VM((R, D), BF16), VM((2, 32, D), BF16),
-            VM((3, 4, R, D), BF16), VM((SLOTS, 1, D), F32),
+            VM((SLOTS, 1, D), F32),
             VM((4, 192, D), BF16), VM((4, 4, 48, D), BF16), VM((4, 4, 48, D), BF16),
             VM((4, 48, D), BF16),
             VM((3, 192, D), BF16), VM((3, 4, 48, D), BF16), VM((3, 4, 48, D), BF16),
             VM((3, 48, D), BF16)]
         + [VM((4, 4, 16, D), BF16)] * 4 + [VM((4, 16, D), F32), VM((3, 3, 16, D), F32)]
         + [dma((6,)), dma((12,)), dma((10,)), dma((2,)), dma((2,)), dma((2,)), dma((3, 2)), dma((2,)),
-           dma((2, 3, SLOTS, 4)), dma((2, 3, SLOTS, 4)), dma((2, 3)), dma((3, 4)), dma((4, 3, 3)), dma((4, 3, 3)),
+           dma((2, 3, SLOTS, 4)), dma((2, 3, SLOTS, 4)), dma((3, 4)), dma((4, 3, 3)), dma((4, 3, 3)),
            dma((2, 4, 4)), dma((2, 4, 4)), dma((3, 3)), dma((3, 3))],
         compiler_params=pltpu.CompilerParams(collective_id=0, has_side_effects=True, vmem_limit_bytes=int(63.4 * 2**20)),
         name="layers",

time: 111 us -> 111 us (level)
  no operation moved by 1% of the time
where the time goes in v1:
time: 111 us
  Pallas kernels  110 us (99%)
    pallas_call x1, Pallas kernels, main(): pl.pallas_call(main_kernel, out_shape=[jax.ShapeDtypeStruct(dims, dtype)...  108 us

profile of v1, /device:TPU:1, one launch (start us, length us, event | category | flops | bytes accessed | tf_op | source)
XLA Modules:
  0.0 110.9 jit_solution(4230184165418600114)
XLA Ops:
  0.6 108.1 %layers.1 = (bf16[2,32,768]{2,1,0:T(8,128)(2,1)}, bf16[2,32,768]{2,1,0:T(8,128)(2,1)}, f32[12,2304]{1,0:T(8,128)}, f32[12,768]{1,0:T(8,128)}, f32[12,3072]{1,0:T...) custom-call(bf16[2,32,768]{2,1,0:T(8,128)(2,1)} %tokens.1, ...), custom_call_target="tpu_custom_call" | custom-call | tf_op jit(solution)/shard_map/layers/pallas_call | solution.py:746
  108.7 2.1 %finish.1 = (bf16[2,32,768]{2,1,0:T(8,128)(2,1)}, bf16[2,32,768]{2,1,0:T(8,128)(2,1)}, f32[12,1,2304]{2,1,0:T(1,128)}, f32[12,1,768]{2,1,0:T(1,128)}, f32[12,1,3...) custom-call(bf16[2,32,768]{2,1,0:T(8,128)(2,1)} %get-tuple-element.2, ...), custom_call_target="tpu_custom_call" | custom-call | tf_op jit(solution)/shard_map/finish/pallas_call | solution.py:801
